TPU v7x, 32 devices: a whole 2x2x4 slice. The times are simulated.
32 devices in a mesh: seq: 8 (over z, y), tp: 4 (over x, core).
Axes of the slice: x: 2, y: 2, z: 4, core: 2. Of those that a mesh axis runs over, the one named last changes fastest.
Arguments:
- tokens: bfloat16 [2048, 1280], P('seq', 'tp'), may hold values from -6 to 6
- first_gain: float32 [1280], replicated, may hold values from 0.1 to 1.9
- w_query: bfloat16 [1280, 1280], P(None, 'tp')
- w_key: bfloat16 [1280, 1280], P(None, 'tp')
- w_value: bfloat16 [1280, 1280], P(None, 'tp'), may hold values from -0.15625 to 0.15625
- w_out: bfloat16 [1280, 1280], P('tp'), may hold values from -0.625 to 0.625
- segment_ids: int32 [2048], P('seq'), may hold values from 0 to 11, never falling along the last dimension, each value on 1 to 512 neighbouring positions
- keep_mask: int32 [2048], P('seq'), may hold values 0 or 1
- merge_gain: float32 [1280], replicated, may hold values from 0.1 to 1.9
- w_merge: bfloat16 [5120, 640], P('tp'), may hold values from -0.078125 to 0.078125
- merge_index: int32 [512, 4], P('seq'), may hold values from 0 to 2047, as said below
- destination: int32 [512], P('seq'), may hold values from 0 to 511, as said below
Outputs:
- delivered: bfloat16 [512, 640], P('seq', 'tp')
Inputs may be any that keep to these rules, and one draw needn't show every extreme that they name: `segment_ids`: segment numbers never fall along the tokens; each picture or clip holds 1 to 512 tokens and one holds exactly 512. `merge_index`: the four entries of merged row m are different tokens of the device that holds row m, that is of rows (m // 64) * 256 to that plus 256 - 1; every token lies in exactly one group. `destination`: a permutation of the merged rows. The owner of row m is destination[m] // 64; the 64 rows of each device go to exactly 8 owners, exactly 8 rows to each.
All inputs are finite; a program needn't handle non-finite values. No bound on the sum of `keep_mask` on one device may be relied on, other than what follows from the above.
Results may differ from a plain program's by a relative error of at most 0.022.
Values may be sent and summed in bfloat16 or wider, within the bound.
A program may use at most 64 MiB of HBM per device.

v0:
```python
import jax
import jax.numpy as jnp
from jax import lax
from jax.sharding import PartitionSpec as P

HD = 80


EPS = 1e-06


def from_behind(shard, axis, by):
    length = lax.axis_size(axis)
    pairs = [(i, i + by) for i in range(length) if 0 <= i + by < length]
    return lax.ppermute(shard, axis, pairs)


def layer_norm(activations, norm_gain):
    activations = activations.astype(jnp.float32)
    row_mean = jnp.mean(activations, axis=-1, keepdims=True)
    centered = activations - row_mean
    variance = jnp.mean(centered * centered, axis=-1, keepdims=True)
    return centered * lax.rsqrt(variance + EPS) * norm_gain


def body(
    tokens,
    first_gain,
    w_query,
    w_key,
    w_value,
    w_out,
    segment_ids,
    keep_mask,
    merge_gain,
    w_merge,
    merge_index,
    destination,
):
    row_count = tokens.shape[0]
    local_width = w_query.shape[1]
    heads_here = local_width // HD
    gathered = lax.all_gather(tokens, "tp", axis=1, tiled=True)
    normed = layer_norm(gathered, first_gain).astype(jnp.bfloat16)
    queries = jnp.dot(normed, w_query, preferred_element_type=jnp.float32).astype(jnp.bfloat16)
    key_rows = jnp.dot(normed, w_key, preferred_element_type=jnp.float32).astype(jnp.bfloat16)
    value_rows = jnp.dot(normed, w_value, preferred_element_type=jnp.float32).astype(jnp.bfloat16)
    paired = jnp.concatenate([key_rows, value_rows], axis=1)
    code_query = segment_ids + 1
    code_key = jnp.where(keep_mask > 0, code_query, 0)
    pair_list = [paired]
    code_list = [code_key]
    for offset in (1, 2, -1, -2):
        moved_pair, moved_code = from_behind((paired, code_key), "seq", offset)
        pair_list.append(moved_pair)
        code_list.append(moved_code)
    all_pairs = jnp.concatenate(pair_list, axis=0)
    all_codes = jnp.concatenate(code_list, axis=0)
    window = all_pairs.shape[0]
    key_heads = all_pairs[:, :local_width].reshape(window, heads_here, HD)
    value_heads = all_pairs[:, local_width:].reshape(window, heads_here, HD)
    query_heads = queries.reshape(row_count, heads_here, HD)
    score_scale = HD ** (-0.5)
    scores = (
        jnp.einsum("qhd,khd->hqk", query_heads, key_heads, preferred_element_type=jnp.float32)
        * score_scale
    )
    query_pos = jnp.arange(row_count)[:, None]
    key_pos = jnp.arange(window)[None, :]
    allowed = (code_query[:, None] == all_codes[None, :]) | (key_pos == query_pos)
    scores = jnp.where(allowed[None], scores, -1e30)
    row_max = jnp.max(scores, axis=-1, keepdims=True)
    exponent = jnp.exp(scores - row_max)
    row_total = jnp.sum(exponent, axis=-1, keepdims=True)
    weights = (exponent / row_total).astype(jnp.bfloat16)
    attended = jnp.einsum("hqk,khd->qhd", weights, value_heads, preferred_element_type=jnp.float32)
    attended = attended.reshape(row_count, local_width).astype(jnp.bfloat16)
    partial_sum = jnp.dot(attended, w_out, preferred_element_type=jnp.float32)
    position = lax.axis_index("tp")
    seq_index = lax.axis_index("seq")
    local_index = merge_index - seq_index * row_count
    column = lax.dynamic_slice_in_dim(local_index, position, 1, 1)[:, 0]
    mixed_sum = lax.psum(partial_sum.astype(jnp.bfloat16), "tp").astype(jnp.float32)
    updated = gathered.astype(jnp.float32) + mixed_sum
    merged_norm = layer_norm(updated, merge_gain).astype(jnp.bfloat16)
    picked = jnp.take(merged_norm, column, axis=0)
    partial_proj = jnp.dot(picked, w_merge, preferred_element_type=jnp.float32)
    projected = lax.psum_scatter(
        partial_proj.astype(jnp.bfloat16), "tp", scatter_dimension=1, tiled=True
    )
    slot_count = projected.shape[0]
    slot_range = jnp.arange(slot_count)
    piece_rows = lax.all_gather(projected, "seq", axis=0, tiled=True)
    piece_dest = lax.all_gather(destination, "seq", axis=0, tiled=True)
    piece_slot = piece_dest - seq_index * slot_count
    one_hot = (piece_slot[None, :] == slot_range[:, None]).astype(jnp.bfloat16)
    delivered = jnp.dot(one_hot, piece_rows, preferred_element_type=jnp.float32)
    return delivered.astype(jnp.bfloat16)


def solution(mesh):
    return jax.shard_map(
        body,
        mesh=mesh,
        in_specs=(
            P("seq", "tp"),
            P(),
            P(None, "tp"),
            P(None, "tp"),
            P(None, "tp"),
            P("tp", None),
            P("seq"),
            P("seq"),
            P(),
            P("tp", None),
            P("seq", None),
            P("seq"),
        ),
        out_specs=P("seq", "tp"),
        check_vma=False,
    )
```

profile of v0, /device:TPU:0, one launch (start us, length us, event | category | flops | bytes accessed | tf_op | source)
XLA Modules:
  0.0 171.0 jit_solution(17523881659542977639)
XLA Ops:
  6.5 9.7 %all_gather.10 = bf16[256,1280]{0,1:T(8,128)(2,1)S(1)} all-gather(bf16[256,320]{0,1:T(8,128)(2,1)} %param.12), channel_id=1, replica_groups=mesh['seq'=8,'tp'=4] {'tp'}, dimensions={1}, use_global_device_ids=true | all-gather | bytes 819200 | tf_op jit(solution)/shard_map/all_gather | solution.py:43
  19.6 4.2 %collective-permute-start = (bf16[256,640]{0,1:T(8,128)(2,1)}, bf16[256,640]{0,1:T(8,128)(2,1)}, u32[]{:S(2)}, u32[]{:S(2)}) collective-permute-start(bf16[256,640]{0,1:T(8,128)(2,1)} %get-tuple-element.11), channel_id=1, source_target_pairs={{0,4},{4,8},{8,12},{12,16},{16,20},{20,24},{24,28},{1,5},{5,9},{9,... | collective-permute-start | bytes 983048 | tf_op jit(solution)/shard_map/ppermute | solution.py:15
  23.8 2.8 %collective-permute-start.1 = (bf16[256,640]{0,1:T(8,128)(2,1)}, bf16[256,640]{0,1:T(8,128)(2,1)S(1)}, u32[]{:S(2)}, u32[]{:S(2)}) collective-permute-start(bf16[256,640]{0,1:T(8,128)(2,1)} %get-tuple-element.11), channel_id=1, source_target_pairs={{0,8},{4,12},{8,16},{12,20},{16,24},{20,28},{1,9},{5,13},{9,17},{1... | collective-permute-start | bytes 983048 | tf_op jit(solution)/shard_map/ppermute | solution.py:15
  26.5 1.3 collective-permute-start.2
  27.8 1.3 collective-permute-start.3
  29.2 4.5 %collective-permute-start.4 = (s32[256]{0:T(256)S(1)}, s32[256]{0:T(256)S(1)}, u32[]{:S(2)}, u32[]{:S(2)}) collective-permute-start(s32[256]{0:T(256)S(1)} %get-tuple-element.8), channel_id=1, source_target_pairs={{0,4},{4,8},{8,12},{12,16},{16,20},{20,24},{24,28},{1,5},{5,9},{9,... | collective-permute-start | bytes 3080 | tf_op jit(solution)/shard_map/ppermute | solution.py:15
  33.7 2.3 %convolution_convert_fusion.1 = bf16[256,320]{0,1:T(8,128)(2,1)} fusion(bf16[1280,320]{0,1:T(8,128)(2,1)} %param.14, bf16[256,1280]{1,0:T(8,128)(2,1)S(1)} %copy.14, f32[1280]{0:T(1024)S(1)} %copy-done.11, f32[256]{0:T(256)S(1)} %add_rsqrt_fusion.1, f32[256]{0:T(256)S(1)} %broadcast_multiply_fusion.1), kind=kOutput, calls=%fused_computation.27 | convolution fusion | flops 211435520 | bytes 1645568 | tf_op jit(solution)/shard_map/dot_general | solution.py:45
  36.1 7.0 %collective-permute-start.5 = (s32[256]{0:T(256)S(1)}, s32[256]{0:T(256)S(1)}, u32[]{:S(2)}, u32[]{:S(2)}) collective-permute-start(s32[256]{0:T(256)S(1)} %get-tuple-element.8), channel_id=1, source_target_pairs={{0,8},{4,12},{8,16},{12,20},{16,24},{20,28},{1,9},{5,13},{9,17},{1... | collective-permute-start | bytes 3080 | tf_op jit(solution)/shard_map/ppermute | solution.py:15
  43.1 1.3 collective-permute-done.5
  44.4 1.3 collective-permute-start.6
  45.7 4.1 %collective-permute-done.6 = s32[256]{0:T(256)S(1)} collective-permute-done((s32[256]{0:T(256)S(1)}, s32[256]{0:T(256)S(1)}, u32[]{:S(2)}, u32[]{:S(2)}) %collective-permute-start.6) | collective-permute-done | bytes 1056 | tf_op jit(solution)/shard_map/ppermute | solution.py:15
  49.8 1.3 collective-permute-start.7
  51.1 4.4 %collective-permute-done.7 = s32[256]{0:T(256)S(1)} collective-permute-done((s32[256]{0:T(256)S(1)}, s32[256]{0:T(256)S(1)}, u32[]{:S(2)}, u32[]{:S(2)}) %collective-permute-start.7) | collective-permute-done | bytes 1056 | tf_op jit(solution)/shard_map/ppermute | solution.py:15
  55.5 1.0 fusion.12
  56.5 1.8 %constant_dynamic-update-slice_fusion.3 = bf16[1280,640]{0,1:T(8,128)(2,1)} fusion(bf16[1280,640]{0,1:T(8,128)(2,1)} %get-tuple-element.12, bf16[256,640]{0,1:T(8,128)(2,1)} %collective-permute-done), kind=kLoop, calls=%fused_computation.42 | loop fusion | bytes 655360
  60.6 2.4 %fusion.33 = (bf16[1280,320]{0,1:T(8,128)(2,1)S(1)}, bf16[1280,320]{0,1:T(8,128)(2,1)}) fusion(bf16[1280,640]{0,1:T(8,128)(2,1)} %constant_dynamic-update-slice_fusion), kind=kLoop, calls=%fused_computation.66 | loop fusion | bytes 3276800 | tf_op jit(solution)/shard_map/slice | solution.py:60
  63.1 3.1 %exponential_reduce_fusion = f32[4,256]{1,0:T(4,128)S(1)} fusion(pred[256,1280]{1,0:T(8,128)(4,1)S(1)} %copy-done.4, bf16[256,4,80]{0,2,1:T(8,128)(2,1)} %bitcast.31, bf16[1280,4,80]{0,2,1:T(8,128)(2,1)S(1)} %bitcast.24), kind=kOutput, calls=%fused_computation.5 | convolution fusion | flops 214959360 | bytes 1314816 | tf_op jit(solution)/shard_map/sub | solution.py:73
  66.2 4.5 %fusion.15 = bf16[4,80,256]{2,1,0:T(8,128)(2,1)} fusion(bf16[1280,4,80]{0,2,1:T(8,128)(2,1)} %bitcast.26, f32[4,256]{1,0:T(4,128)S(1)} %exponential_reduce_fusion, pred[256,1280]{1,0:T(8,128)(4,1)S(1)} %copy-done.4, bf16[256,4,80]{0,2,1:T(8,128)(2,1)} %bitcast.32, bf16[1280,4,80]{0,2,1:T(8,128)(2,1)} %bitcast.25), kind=kOutput, calls=%fused_computation.26 | convolution fusion | flops 426068224 | bytes 2297856 | tf_op jit(solution)/shard_map/hqk,khd->qhd/dot_general | solution.py:76
  70.7 2.3 %convolution_convert_fusion = bf16[256,1280]{1,0:T(8,128)(2,1)} fusion(bf16[256,320]{0,1:T(8,128)(2,1)} %bitcast.28, bf16[320,1280]{1,0:T(8,128)(2,1)S(1)} %copy-done.2), kind=kOutput, calls=%fused_computation.11 | convolution fusion | flops 210042880 | bytes 1638400 | tf_op jit(solution)/shard_map/dot_general | solution.py:78
  74.7 10.2 %all-reduce = s32[512]{0:T(512)S(1)} all-reduce(s32[512]{0:T(512)S(1)} %dynamic-update-slice), channel_id=1, replica_groups=mesh['seq'=8,'tp'=4] {'seq'}, use_global_device_ids=true, to_apply=%add | all-reduce | flops 512 | bytes 4096
  84.9 22.7 %all-reduce.3.cloned.1.call-done = bf16[256,1280]{1,0:T(8,128)(2,1)} async-done(((bf16[256,1280]{1,0:T(8,128)(2,1)}), bf16[256,1280]{1,0:T(8,128)(2,1)}) %all-reduce.3.cloned.1.call-update) | async-done | bytes 655376 | tf_op jit(solution)/shard_map/psum | solution.py:83
  107.6 1.4 fusion.14
  111.8 19.8 %reduce-scatter.4.cloned.1.call-done = bf16[160,64]{1,0:T(8,128)(2,1)} async-done(((bf16[640,64]{1,0:T(8,128)(2,1)}), bf16[160,64]{1,0:T(8,128)(2,1)}) %reduce-scatter.4.cloned.1.call-update) | async-done | bytes 20496
  132.4 31.0 %all_gather.11 = bf16[512,160]{1,0:T(8,128)(2,1)S(1)} all-gather(bf16[64,160]{1,0:T(8,128)(2,1)S(1)} %copy.16), channel_id=1, replica_groups=mesh['seq'=8,'tp'=4] {'seq'}, dimensions={0}, use_global_device_ids=true | all-gather | bytes 184320 | tf_op jit(solution)/shard_map/all_gather | solution.py:93
  (70 shorter events, 11.0 us)
Async XLA Ops:
  6.5 103.9 %copy-start = (bf16[1280,640]{1,0:T(8,128)(2,1)S(1)}, bf16[1280,640]{1,0:T(8,128)(2,1)}, u32[]{:S(2)}) copy-start(bf16[1280,640]{1,0:T(8,128)(2,1)} %param.21) | copy-start | bytes 4915204
  6.5 101.1 %all-reduce.3.cloned.1.call-start = ((), (), s32[]{:S(2)}) async-start(), calls=%async_computation.1 | async-start | bytes 1310720 | tf_op jit(solution)/shard_map/psum | solution.py:83
  16.2 0.8 copy-start.11
  16.4 1.1 copy-start.9
  17.0 1.2 copy-start.10
  18.2 11.0 %copy-start.7 = (s32[256]{0:T(256)S(1)}, s32[256]{0:T(256)}, u32[]{:S(2)}) copy-start(s32[256]{0:T(256)} %param.18) | copy-start | bytes 3076
  18.2 11.0 %copy-start.8 = (s32[256]{0:T(256)S(1)}, s32[256]{0:T(256)}, u32[]{:S(2)}) copy-start(s32[256]{0:T(256)} %param.19) | copy-start | bytes 3076
  19.6 36.9 %collective-permute-start = (bf16[256,640]{0,1:T(8,128)(2,1)}, bf16[256,640]{0,1:T(8,128)(2,1)}, u32[]{:S(2)}, u32[]{:S(2)}) collective-permute-start(bf16[256,640]{0,1:T(8,128)(2,1)} %get-tuple-element.11), channel_id=1, source_target_pairs={{0,4},{4,8},{8,12},{12,16},{16,20},{20,24},{24,28},{1,5},{5,9},{9,... | collective-permute-start | bytes 983048 | tf_op jit(solution)/shard_map/ppermute | solution.py:15
  23.8 34.5 %collective-permute-start.1 = (bf16[256,640]{0,1:T(8,128)(2,1)}, bf16[256,640]{0,1:T(8,128)(2,1)S(1)}, u32[]{:S(2)}, u32[]{:S(2)}) collective-permute-start(bf16[256,640]{0,1:T(8,128)(2,1)} %get-tuple-element.11), channel_id=1, source_target_pairs={{0,8},{4,12},{8,16},{12,20},{16,24},{20,28},{1,9},{5,13},{9,17},{1... | collective-permute-start | bytes 983048 | tf_op jit(solution)/shard_map/ppermute | solution.py:15
  26.5 32.5 %collective-permute-start.2 = (bf16[256,640]{0,1:T(8,128)(2,1)}, bf16[256,640]{0,1:T(8,128)(2,1)S(1)}, u32[]{:S(2)}, u32[]{:S(2)}) collective-permute-start(bf16[256,640]{0,1:T(8,128)(2,1)} %get-tuple-element.11), channel_id=1, source_target_pairs={{4,0},{8,4},{12,8},{16,12},{20,16},{24,20},{28,24},{5,1},{9,5},{13... | collective-permute-start | bytes 983048 | tf_op jit(solution)/shard_map/ppermute | solution.py:15
  27.8 32.0 %collective-permute-start.3 = (bf16[256,640]{0,1:T(8,128)(2,1)}, bf16[256,640]{0,1:T(8,128)(2,1)S(1)}, u32[]{:S(2)}, u32[]{:S(2)}) collective-permute-start(bf16[256,640]{0,1:T(8,128)(2,1)} %get-tuple-element.11), channel_id=1, source_target_pairs={{8,0},{12,4},{16,8},{20,12},{24,16},{28,20},{9,1},{13,5},{17,9},{2... | collective-permute-start | bytes 983048 | tf_op jit(solution)/shard_map/ppermute | solution.py:15
  29.2 6.9 %collective-permute-start.4 = (s32[256]{0:T(256)S(1)}, s32[256]{0:T(256)S(1)}, u32[]{:S(2)}, u32[]{:S(2)}) collective-permute-start(s32[256]{0:T(256)S(1)} %get-tuple-element.8), channel_id=1, source_target_pairs={{0,4},{4,8},{8,12},{12,16},{16,20},{20,24},{24,28},{1,5},{5,9},{9,... | collective-permute-start | bytes 3080 | tf_op jit(solution)/shard_map/ppermute | solution.py:15
  36.1 8.3 %collective-permute-start.5 = (s32[256]{0:T(256)S(1)}, s32[256]{0:T(256)S(1)}, u32[]{:S(2)}, u32[]{:S(2)}) collective-permute-start(s32[256]{0:T(256)S(1)} %get-tuple-element.8), channel_id=1, source_target_pairs={{0,8},{4,12},{8,16},{12,20},{16,24},{20,28},{1,9},{5,13},{9,17},{1... | collective-permute-start | bytes 3080 | tf_op jit(solution)/shard_map/ppermute | solution.py:15
  44.4 5.5 %collective-permute-start.6 = (s32[256]{0:T(256)S(1)}, s32[256]{0:T(256)S(1)}, u32[]{:S(2)}, u32[]{:S(2)}) collective-permute-start(s32[256]{0:T(256)S(1)} %get-tuple-element.8), channel_id=1, source_target_pairs={{4,0},{8,4},{12,8},{16,12},{20,16},{24,20},{28,24},{5,1},{9,5},{13... | collective-permute-start | bytes 3080 | tf_op jit(solution)/shard_map/ppermute | solution.py:15
  49.8 5.7 %collective-permute-start.7 = (s32[256]{0:T(256)S(1)}, s32[256]{0:T(256)S(1)}, u32[]{:S(2)}, u32[]{:S(2)}) collective-permute-start(s32[256]{0:T(256)S(1)} %get-tuple-element.8), channel_id=1, source_target_pairs={{8,0},{12,4},{16,8},{20,12},{24,16},{28,20},{9,1},{13,5},{17,9},{2... | collective-permute-start | bytes 3080 | tf_op jit(solution)/shard_map/ppermute | solution.py:15
  60.6 2.4 %copy-start.4 = (pred[256,1280]{1,0:T(8,128)(4,1)S(1)}, pred[256,1280]{1,0:T(8,128)(4,1)}, u32[]{:S(2)}) copy-start(pred[256,1280]{1,0:T(8,128)(4,1)} %fusion.12) | copy-start | bytes 983044
  63.1 3.1 %copy-start.3 = (bf16[1280,320]{0,1:T(8,128)(2,1)}, bf16[1280,320]{0,1:T(8,128)(2,1)S(1)}, u32[]{:S(2)}) copy-start(bf16[1280,320]{0,1:T(8,128)(2,1)S(1)} %get-tuple-element.9) | copy-start | bytes 2457604
  66.2 4.5 %copy-start.2 = (bf16[320,1280]{1,0:T(8,128)(2,1)S(1)}, bf16[320,1280]{1,0:T(8,128)(2,1)}, u32[]{:S(2)}) copy-start(bf16[320,1280]{1,0:T(8,128)(2,1)} %param.17) | copy-start | bytes 2457604
  70.7 2.4 %copy-start.6 = (s32[64,4]{0,1:T(4,128)S(1)}, s32[64,4]{0,1:T(4,128)}, u32[]{:S(2)}) copy-start(s32[64,4]{0,1:T(4,128)} %param.22) | copy-start | bytes 3076
  70.7 2.4 %copy-start.13 = (u32[32]{0:T(128)S(1)}, u32[32]{0:T(128)}, u32[]{:S(2)}) copy-start(u32[32]{0:T(128)} %constant.52) | copy-start | bytes 388
  70.7 3.7 %copy-start.12 = (s32[64]{0:T(128)S(1)}, s32[64]{0:T(128)}, u32[]{:S(2)}) copy-start(s32[64]{0:T(128)} %param.23) | copy-start | bytes 772
  73.1 58.5 %reduce-scatter.4.cloned.1.call-start = ((), (), s32[]{:S(2)}) async-start(), calls=%async_computation.2 | async-start | bytes 204800
  84.9 24.5 %copy-start.5 = (f32[1280]{0:T(1024)S(1)}, f32[1280]{0:T(1024)}, u32[]{:S(2)}) copy-start(f32[1280]{0:T(1024)} %param.20) | copy-start | bytes 15364
  107.6 1.4 copy-start.1
Sparse Core Ops, SparseCore 0:
  73.2 34.3 all-reduce.2
  111.9 19.6 reduce-scatter.3
where the time goes:
time: 172 us; the launch traced here: 171 us
  waiting for transfers between devices  52.4 us (30%)
  blocking collectives  50.9 us (30%)
  starting transfers between devices  23.7 us (14%)
  matrix products  14.5 us (8%)
  between operations  14.4 us (8%)
  local copies, waits for them, and re-layouts  10.8 us (6%)
  other arithmetic  4.5 us (3%)
    all_gather x1, blocking collectives, body(): piece_rows = lax.all_gather(projected, 'seq', axis=0, tiled=True)  31 us
    ppermute x8, starting transfers between devices, from_behind(): return lax.ppermute(shard, axis, pairs)  23.6 us
    psum x1, waiting for transfers between devices, body(): lax.psum(partial_sum.astype(jnp.bfloat16), 'tp').astype(jnp.float32)  22.7 us
    unnamed x3, waiting for transfers between devices  19.8 us
    unnamed x1, blocking collectives  10.2 us
    ppermute x8, waiting for transfers between devices, from_behind(): return lax.ppermute(shard, axis, pairs)  9.84 us
    all_gather x1, blocking collectives, body(): gathered = lax.all_gather(tokens, 'tp', axis=1, tiled=True)  9.66 us
    unnamed x39, local copies, waits for them, and re-layouts  6.55 us
  transfers between devices with their start and end apart: 10, of which 5 were waited for; matrix products, arithmetic and copies ran while one was open for 4% of the time, Pallas kernels for 0%

commit v1 on v0

v1 whole, which is shorter than its diff:
```python
import functools

import jax
import jax.numpy as jnp
from jax import lax
from jax.experimental import pallas as pl
from jax.experimental.pallas import tpu as pltpu
from jax.sharding import PartitionSpec as P

HD = 80
EPS = 1e-06
LOG2E = 1.4426950408889634
MESH = pl.DeviceIdType.MESH
OFFSETS = (1, -1, 2, -2)
KEY_WINDOW = (0, 0, 128, 128)
VALUE_WINDOW = (256, 256, 384, 384)
F32 = jnp.float32
BF16 = jnp.bfloat16


def normalise(rows, gain):
    mean = jnp.mean(rows, axis=-1, keepdims=True)
    centered = rows - mean
    variance = jnp.mean(centered * centered, axis=-1, keepdims=True)
    return centered * lax.rsqrt(variance + EPS) * gain


def kernel(
    n, tp,
    tokens, first_gain, w_query, w_key, w_value, w_out, segments, keep,
    merge_gain, w_merge, merge_index, destination,
    out,
    gathered, wq, wk, wv, wo, wm, pairs, codes, dests, queries,
    part_send, part_recv, proj_send, proj_recv, rows,
    local_sem, tok_send, tok_recv, pair_send, pair_recv, code_send, code_recv,
    dest_send, dest_recv, part_ssem, part_rsem, proj_ssem, proj_rsem, row_send, row_recv,
):
    s, t = lax.axis_index("seq"), lax.axis_index("tp")
    count = tokens.shape[0]
    width = tokens.shape[1]
    merged = merge_index.shape[0]

    barrier = pltpu.get_barrier_semaphore()
    for d in range(1, tp):
        pl.semaphore_signal(barrier, inc=1, device_id=(s, lax.rem(t + d, tp)), device_id_type=MESH)

    @pl.loop(1, n)
    def _(d):
        pl.semaphore_signal(barrier, inc=1, device_id=(lax.rem(s + d, n), t), device_id_type=MESH)

    half = w_out.shape[0] // 2
    local = [
        pltpu.make_async_copy(tokens, gathered.at[t], local_sem.at[0]),
        pltpu.make_async_copy(w_key, wk, local_sem.at[1]),
        pltpu.make_async_copy(w_value, wv, local_sem.at[2]),
        pltpu.make_async_copy(w_query, wq, local_sem.at[3]),
        pltpu.make_async_copy(w_out.at[pl.ds(0, half)], wo.at[pl.ds(64, half)], local_sem.at[4]),
        pltpu.make_async_copy(w_out.at[pl.ds(half, half)], wo.at[pl.ds(352, half)], local_sem.at[5]),
        pltpu.make_async_copy(w_merge, wm, local_sem.at[6]),
    ]
    for copy in local:
        copy.start()
    wo[0:64, :] = jnp.zeros((64, wo.shape[1]), BF16)
    wo[224:352, :] = jnp.zeros((128, wo.shape[1]), BF16)
    code_query = segments[...] + 1
    codes[0] = jnp.where(keep[...] > 0, code_query, 0)
    dests[s] = destination[...]

    pl.semaphore_wait(barrier, tp - 1 + n - 1)

    def tok_copy(d):
        return pltpu.make_async_remote_copy(
            src_ref=tokens, dst_ref=gathered.at[t],
            send_sem=tok_send.at[d], recv_sem=tok_recv.at[d],
            device_id=(s, lax.rem(t + d, tp)), device_id_type=MESH)

    for d in range(1, tp):
        tok_copy(d).start()

    def code_copy(i):
        return pltpu.make_async_remote_copy(
            src_ref=codes.at[0], dst_ref=codes.at[i + 1],
            send_sem=code_send.at[i], recv_sem=code_recv.at[i],
            device_id=(s + OFFSETS[i], t), device_id_type=MESH)

    def pair_copy(i):
        return pltpu.make_async_remote_copy(
            src_ref=pairs.at[0], dst_ref=pairs.at[i + 1],
            send_sem=pair_send.at[i], recv_sem=pair_recv.at[i],
            device_id=(s + OFFSETS[i], t), device_id_type=MESH)

    def has(offset):
        return (s + offset >= 0) & (s + offset < n)

    for i, o in enumerate(OFFSETS):
        @pl.when(has(o))
        def _():
            code_copy(i).start()

    def dest_copy(d):
        return pltpu.make_async_remote_copy(
            src_ref=dests.at[s], dst_ref=dests.at[s],
            send_sem=dest_send.at[d], recv_sem=dest_recv.at[d],
            device_id=(lax.rem(s + d, n), t), device_id_type=MESH)

    @pl.loop(1, n)
    def _(d):
        dest_copy(d).start()

    for i, o in enumerate(OFFSETS):
        @pl.when(jnp.logical_not(has(-o)))
        def _():
            pairs[i + 1] = jnp.zeros(pairs.shape[1:], BF16)
            codes[i + 1] = jnp.zeros(codes.shape[1:], jnp.int32)

    token_lane = lax.broadcasted_iota(jnp.int32, (merged, count), 1)
    index = merge_index[...] - s * count
    picks = [(index[:, j:j + 1] == token_lane).astype(BF16) for j in range(tp)]
    pick_all = jnp.concatenate(picks, axis=0)
    pos_lane = lax.broadcasted_iota(jnp.int32, index.shape, 1)
    mine = jnp.sum(jnp.where(pos_lane == t, index, 0), axis=1, keepdims=True)
    pick_mine = (mine == token_lane).astype(BF16)
    diag = lax.broadcasted_iota(jnp.int32, (count, count), 0) == lax.broadcasted_iota(jnp.int32, (count, count), 1)
    code_column = jnp.sum(jnp.where(diag, code_query, 0), axis=1, keepdims=True)

    for d in range(1, tp):
        tok_copy(d).wait_recv()
    local[0].wait()
    whole = jnp.concatenate([gathered[j].astype(F32) for j in range(tp)], axis=1)
    residual = jnp.dot(pick_mine, whole.astype(BF16), preferred_element_type=F32)
    normed = normalise(whole, first_gain[...]).astype(BF16)
    local[1].wait()
    local[2].wait()
    pairs[0] = jnp.concatenate(
        [jnp.dot(normed, wk[...], preferred_element_type=F32),
         jnp.dot(normed, wv[...], preferred_element_type=F32)], axis=1).astype(BF16)
    for i, o in enumerate(OFFSETS):
        @pl.when(has(o))
        def _():
            pair_copy(i).start()

    local[3].wait()
    q = jnp.dot(normed, wq[...], preferred_element_type=F32)
    queries[...] = jnp.concatenate([q, jnp.zeros((count, 64), F32)], axis=1).astype(BF16)
    lane = lax.broadcasted_iota(jnp.int32, (count, 256), 1)
    head_q = []
    for h in range(4):
        start = KEY_WINDOW[h]
        inside = (lane + start >= h * HD) & (lane + start < (h + 1) * HD)
        head_q.append(jnp.where(inside, queries[:, start:start + 256], jnp.zeros((), BF16)))

    factor = HD ** (-0.5) * LOG2E
    state = [None] * 4
    for b in range(5):
        if b:
            i = b - 1

            @pl.when(has(-OFFSETS[i]))
            def _():
                code_copy(i).wait_recv()
                pair_copy(i).wait_recv()
        allowed = code_column == codes[b]
        if b == 0:
            allowed = allowed | diag
        for h in range(4):
            key = pairs[b, :, KEY_WINDOW[h]:KEY_WINDOW[h] + 256]
            value = pairs[b, :, VALUE_WINDOW[h]:VALUE_WINDOW[h] + 256]
            scores = lax.dot_general(head_q[h], key, (((1,), (1,)), ((), ())), preferred_element_type=F32)
            scores = jnp.where(allowed, scores * factor, -1e30)
            top = jnp.max(scores, axis=1, keepdims=True)
            if b:
                top = jnp.maximum(top, state[h][0])
            expo = jnp.exp2(scores - top)
            total = jnp.sum(expo, axis=1, keepdims=True)
            acc = jnp.dot(expo.astype(BF16), value, preferred_element_type=F32)
            if b:
                shrink = jnp.exp2(state[h][0] - top)
                total = total + shrink * state[h][1]
                acc = acc + shrink * state[h][2]
            state[h] = (top, total, acc)

    heads = [acc / total for _, total, acc in state]
    attended = jnp.concatenate(
        [jnp.where(lane < 144, heads[0], heads[1]), jnp.where(lane < 176, heads[2], heads[3])],
        axis=1).astype(BF16)
    attended = jnp.dot(pick_all, attended, preferred_element_type=F32).astype(BF16)
    local[4].wait()
    local[5].wait()

    def part_copy(d):
        peer = lax.rem(t + d, tp)
        return pltpu.make_async_remote_copy(
            src_ref=part_send.at[peer], dst_ref=part_recv.at[d],
            send_sem=part_ssem.at[d], recv_sem=part_rsem.at[d],
            device_id=(s, peer), device_id_type=MESH)

    part = jnp.dot(attended, wo[...], preferred_element_type=F32).astype(BF16)
    for j in range(tp):
        part_send[j] = part[j * merged:(j + 1) * merged]
    for d in range(1, tp):
        part_copy(d).start()
    updated = residual + part_send[t].astype(F32)
    for d in range(1, tp):
        part_copy(d).wait_recv()
        updated = updated + part_recv[d].astype(F32)
    merged_norm = normalise(updated, merge_gain[...]).astype(BF16)
    local[6].wait()
    proj = jnp.dot(merged_norm, wm[...], preferred_element_type=F32)
    piece = proj.shape[1] // tp
    for j in range(tp):
        proj_send[j] = proj[:, j * piece:(j + 1) * piece].astype(BF16)

    def proj_copy(d):
        peer = lax.rem(t + d, tp)
        return pltpu.make_async_remote_copy(
            src_ref=proj_send.at[peer], dst_ref=proj_recv.at[d],
            send_sem=proj_ssem.at[d], recv_sem=proj_rsem.at[d],
            device_id=(s, peer), device_id_type=MESH)

    for d in range(1, tp):
        proj_copy(d).start()
    projected = proj_send[t].astype(F32)
    for d in range(1, tp):
        proj_copy(d).wait_recv()
        projected = projected + proj_recv[d].astype(F32)
    rows[s] = projected.astype(BF16)

    def row_copy(d):
        return pltpu.make_async_remote_copy(
            src_ref=rows.at[s], dst_ref=rows.at[s],
            send_sem=row_send.at[d], recv_sem=row_recv.at[d],
            device_id=(lax.rem(s + d, n), t), device_id_type=MESH)

    @pl.loop(1, n)
    def _(d):
        row_copy(d).start()

    slot = lax.broadcasted_iota(jnp.int32, (merged, merged), 0)

    def deliver(source):
        one_hot = ((dests[source] - s * merged) == slot).astype(BF16)
        return jnp.dot(one_hot, rows[source], preferred_element_type=F32)

    def step(d, total):
        dest_copy(d).wait_recv()
        row_copy(d).wait_recv()
        return total + deliver(lax.rem(s + n - d, n))

    total = lax.fori_loop(1, n, step, deliver(s))
    out[...] = total.astype(BF16)

    for d in range(1, tp):
        tok_copy(d).wait_send()
        part_copy(d).wait_send()
        proj_copy(d).wait_send()
    for i, o in enumerate(OFFSETS):
        @pl.when(has(o))
        def _():
            code_copy(i).wait_send()
            pair_copy(i).wait_send()

    @pl.loop(1, n)
    def _(d):
        dest_copy(d).wait_send()
        row_copy(d).wait_send()


def body(n, tp, tokens, first_gain, w_query, w_key, w_value, w_out, segment_ids, keep_mask,
         merge_gain, w_merge, merge_index, destination):
    count, width = tokens.shape
    features = w_query.shape[0]
    merged = merge_index.shape[0]
    piece = w_merge.shape[1] // tp
    anywhere = pl.BlockSpec(memory_space=pl.ANY)
    vmem = pl.BlockSpec(memory_space=pltpu.VMEM)
    dma = pltpu.SemaphoreType.DMA
    return pl.pallas_call(
        functools.partial(kernel, n, tp),
        out_shape=jax.ShapeDtypeStruct((merged, piece), BF16),
        in_specs=[anywhere, vmem, anywhere, anywhere, anywhere, anywhere, vmem, vmem, vmem, anywhere, vmem, vmem],
        out_specs=vmem,
        scratch_shapes=[
            pltpu.VMEM((tp, count, width), BF16),
            pltpu.VMEM(w_query.shape, BF16),
            pltpu.VMEM(w_key.shape, BF16),
            pltpu.VMEM(w_value.shape, BF16),
            pltpu.VMEM((512, features), BF16),
            pltpu.VMEM(w_merge.shape, BF16),
            pltpu.VMEM((5, count, 2 * width), BF16),
            pltpu.VMEM((5, 1, count), jnp.int32),
            pltpu.VMEM((n, 1, merged), jnp.int32),
            pltpu.VMEM((count, 384), BF16),
            pltpu.VMEM((tp, merged, features), BF16),
            pltpu.VMEM((tp, merged, features), BF16),
            pltpu.VMEM((tp, merged, piece), BF16),
            pltpu.VMEM((tp, merged, piece), BF16),
            pltpu.VMEM((n, merged, piece), BF16),
            dma((7,)),
            dma((tp,)), dma((tp,)),
            dma((4,)), dma((4,)), dma((4,)), dma((4,)),
            dma((n,)), dma((n,)),
            dma((tp,)), dma((tp,)), dma((tp,)), dma((tp,)),
            dma((n,)), dma((n,)),
        ],
        compiler_params=pltpu.CompilerParams(
            collective_id=0, has_side_effects=True, vmem_limit_bytes=56 * 1024 * 1024),
        name="vision_layer",
    )(tokens, first_gain.reshape(1, -1), w_query, w_key, w_value, w_out,
      segment_ids.reshape(1, -1), keep_mask.reshape(1, -1), merge_gain.reshape(1, -1),
      w_merge, merge_index, destination.reshape(1, -1))


def solution(mesh):
    n, tp = mesh.shape["seq"], mesh.shape["tp"]
    return jax.shard_map(
        functools.partial(body, n, tp),
        mesh=mesh,
        in_specs=(
            P("seq", "tp"), P(), P(None, "tp"), P(None, "tp"), P(None, "tp"), P("tp", None),
            P("seq"), P("seq"), P(), P("tp", None), P("seq", None), P("seq"),
        ),
        out_specs=P("seq", "tp"),
        check_vma=False,
    )
```

time: 172 us -> 66.2 us (0.38)
  Pallas kernels: 0 us -> 53.8 us
  waiting for transfers between devices: 52.4 us -> 0 us
  blocking collectives: 50.9 us -> 0 us
  starting transfers between devices: 23.7 us -> 0 us
  matrix products: 14.5 us -> 0 us
  between operations: 14.4 us -> 0.01 us
  other arithmetic: 4.5 us -> 0 us
    pallas_call x0 -> x1, Pallas kernels: none -> 53.8 us  [body(): pl.pallas_call(functools.partial(kernel, n, tp), out_shape=jax.ShapeDtype...]
    all_gather x2 -> x0, blocking collectives: 40.6 us -> none  [the longest x1 31 us: body(): piece_rows = lax.all_gather(projected, 'seq', axis=0, tiled=True)]
    ppermute x8 -> x0, starting transfers between devices: 23.6 us -> none  [from_behind(): return lax.ppermute(shard, axis, pairs)]
    psum x1 -> x0, waiting for transfers between devices: 22.7 us -> none  [body(): lax.psum(partial_sum.astype(jnp.bfloat16), 'tp').astype(jnp.float32)]
    unnamed x3 -> x0, waiting for transfers between devices: 19.8 us -> none
    dot_general x7 -> x0, matrix products: 11.4 us -> none  [the longest x1 4.51 us: body(): jnp.einsum('hqk,khd->qhd', weights, value_heads, preferred_element_type=j...]
    unnamed x1 -> x0, blocking collectives: 10.2 us -> none
    ppermute x8 -> x0, waiting for transfers between devices: 9.84 us -> none  [from_behind(): return lax.ppermute(shard, axis, pairs)]
  transfers between devices with their start and end apart: 10 -> 0, of which waited for: 5 -> 0; matrix products, arithmetic and copies ran while one was open for 4% -> 0% of each run, Pallas kernels for 0% -> 0%
where the time goes in v1:
time: 66.2 us; the launch traced here: 65.8 us
  Pallas kernels  53.8 us (81%)
  local copies, waits for them, and re-layouts  12 us (18%)
    pallas_call x1, Pallas kernels, body(): pl.pallas_call(functools.partial(kernel, n, tp), out_shape=jax.ShapeDtype...  53.8 us
    unnamed x10, local copies, waits for them, and re-layouts  9.39 us
    reshape x1, local copies, waits for them, and re-layouts, body(): first_gain.reshape(1, -1)  1.37 us

profile of v1, /device:TPU:0, one launch (start us, length us, event | category | flops | bytes accessed | tf_op | source)
XLA Modules:
  0.0 65.8 jit_solution(6501888514318153381)
XLA Ops:
  0.0 0.0 copy-start
  0.0 1.4 %reshape.15.first_gain = f32[1,1280]{1,0:T(1,128)} reshape(f32[1280]{0:T(1024)} %param.13) | data formatting | bytes 10240 | tf_op jit(solution)/shard_map/reshape | solution.py:308
  1.4 1.3 %reshape.18.merge_gain = f32[1,1280]{1,0:T(1,128)} reshape(f32[1280]{0:T(1024)} %param.20) | data formatting | bytes 10240 | tf_op jit(solution)/shard_map/reshape | solution.py:309
  2.6 1.4 %copy.17.merge_index = s32[64,4]{1,0:T(8,128)} copy(s32[64,4]{0,1:T(4,128)} %param.22) | data formatting | bytes 2048 | tf_op args[10]
  4.0 1.7 %copy.13.tokens = bf16[256,320]{1,0:T(8,128)(2,1)} copy(bf16[256,320]{0,1:T(8,128)(2,1)} %param.12) | data formatting | bytes 327680 | tf_op args[0]
  5.8 0.0 copy-start.1
  5.8 2.3 %copy.14.w_query = bf16[1280,320]{1,0:T(8,128)(2,1)} copy(bf16[1280,320]{0,1:T(8,128)(2,1)} %param.14) | data formatting | bytes 1638400 | tf_op args[2]
  8.1 0.0 copy-done
  8.1 1.3 %copy.15.w_key = bf16[1280,320]{1,0:T(8,128)(2,1)} copy(bf16[1280,320]{0,1:T(8,128)(2,1)S(1)} %copy-done) | data formatting | bytes 1638400 | tf_op args[3]
  9.4 0.0 copy-done.1
  9.4 1.3 %copy.16.w_value = bf16[1280,320]{1,0:T(8,128)(2,1)} copy(bf16[1280,320]{0,1:T(8,128)(2,1)S(1)} %copy-done.1) | data formatting | bytes 1638400 | tf_op args[4]
  10.7 53.8 %vision_layer.1 = bf16[64,160]{1,0:T(8,128)(2,1)} custom-call(bf16[256,320]{1,0:T(8,128)(2,1)} %copy.13.tokens, f32[1,1280]{1,0:T(1,128)} %reshape.15.first_gain, bf16[1280,320]{1,0:T(8,128)(2,1)} %copy.14.w_query, bf16[1280,320]{1,0:T(8,128)(2,1)} %copy.15.w_key, bf16[1280,320]{1,0:T(8,128)(2,1)} %copy.16.w_value, bf16[320,1280]{1,0:T(8,128)(2,1)} %w_out.1, ...), custom_call_target="tpu_custom_call" | custom-call | tf_op jit(solution)/shard_map/vision_layer/pallas_call | solution.py:277
  64.4 1.4 %copy.19 = bf16[64,160]{1,0:T(8,128)(2,1)} copy(bf16[64,160]{1,0:T(8,128)(2,1)} %vision_layer.1) | data formatting | bytes 40960
Async XLA Ops:
  0.0 8.1 %copy-start = (bf16[1280,320]{0,1:T(8,128)(2,1)S(1)}, bf16[1280,320]{0,1:T(8,128)(2,1)}, u32[]{:S(2)}) copy-start(bf16[1280,320]{0,1:T(8,128)(2,1)} %param.15) | copy-start | bytes 2457604
  5.8 3.6 %copy-start.1 = (bf16[1280,320]{0,1:T(8,128)(2,1)S(1)}, bf16[1280,320]{0,1:T(8,128)(2,1)}, u32[]{:S(2)}) copy-start(bf16[1280,320]{0,1:T(8,128)(2,1)} %param.16) | copy-start | bytes 2457604

commit v2 on v1

v2 whole, which is shorter than its diff:
```python
import functools

import jax
import jax.numpy as jnp
from jax import lax
from jax.experimental import pallas as pl
from jax.experimental.pallas import tpu as pltpu
from jax.sharding import PartitionSpec as P

HD = 80
EPS = 1e-06
LOG2E = 1.4426950408889634
MESH = pl.DeviceIdType.MESH
OFFSETS = (1, -1, 2, -2)
F32 = jnp.float32
BF16 = jnp.bfloat16


def normalise(rows, gain, axis):
    mean = jnp.mean(rows, axis=axis, keepdims=True)
    centered = rows - mean
    variance = jnp.mean(centered * centered, axis=axis, keepdims=True)
    return centered * lax.rsqrt(variance + EPS) * gain


def kernel(
    n, tp,
    tokens, first_gain, w_query, w_key, w_value, w_out, segments, keep,
    merge_gain, w_merge, merge_index, destination,
    out,
    gathered, wq, wk, wv, wo, wm, pairs, codes, dests, queries,
    picks, part_send, part_recv, proj_send, proj_recv, rows,
    local_sem, tok_send, tok_recv, pair_send, pair_recv, code_send, code_recv,
    dest_send, dest_recv, part_ssem, part_rsem, proj_ssem, proj_rsem, row_send, row_recv,
):
    s, t = lax.axis_index("seq"), lax.axis_index("tp")
    width, count = tokens.shape
    merged = merge_index.shape[1]
    beside, across, far = t + 1 - 2 * lax.rem(t, 2), lax.rem(t + 2, 4), 3 - t

    barrier = pltpu.get_barrier_semaphore()
    for d in range(1, tp):
        pl.semaphore_signal(barrier, inc=1, device_id=(s, lax.rem(t + d, tp)), device_id_type=MESH)

    @pl.loop(1, n)
    def _(d):
        pl.semaphore_signal(barrier, inc=1, device_id=(lax.rem(s + d, n), t), device_id_type=MESH)

    local = [
        pltpu.make_async_copy(tokens, gathered.at[t], local_sem.at[0]),
        pltpu.make_async_copy(w_key, wk, local_sem.at[1]),
        pltpu.make_async_copy(w_value, wv, local_sem.at[2]),
        pltpu.make_async_copy(w_query, wq, local_sem.at[3]),
        pltpu.make_async_copy(w_out, wo, local_sem.at[4]),
        pltpu.make_async_copy(w_merge, wm, local_sem.at[5]),
    ]
    for copy in local:
        copy.start()
    code_query = segments[...] + 1
    codes[0] = jnp.where(keep[...] > 0, code_query, 0)
    dests[s] = destination[...]

    pl.semaphore_wait(barrier, tp - 1 + n - 1)

    half = width // 2

    def tok_copy(i):
        if i == 2:
            source, target, peer = tokens, gathered.at[t], beside
        elif i < 2:
            part = pl.ds(i * half, half)
            source, target, peer = tokens.at[part], gathered.at[t, part], across
        else:
            part = pl.ds((i - 3) * half, half)
            source = gathered.at[across, part]
            target, peer = source, beside
        return pltpu.make_async_remote_copy(
            src_ref=source, dst_ref=target, send_sem=tok_send.at[i], recv_sem=tok_recv.at[i],
            device_id=(s, peer), device_id_type=MESH)

    for i in range(3):
        tok_copy(i).start()

    def code_copy(i):
        return pltpu.make_async_remote_copy(
            src_ref=codes.at[0], dst_ref=codes.at[i + 1],
            send_sem=code_send.at[i], recv_sem=code_recv.at[i],
            device_id=(s + OFFSETS[i], t), device_id_type=MESH)

    def pair_copy(i):
        return pltpu.make_async_remote_copy(
            src_ref=pairs.at[0], dst_ref=pairs.at[i + 1],
            send_sem=pair_send.at[i], recv_sem=pair_recv.at[i],
            device_id=(s + OFFSETS[i], t), device_id_type=MESH)

    def has(offset):
        return (s + offset >= 0) & (s + offset < n)

    for i, o in enumerate(OFFSETS):
        @pl.when(has(o))
        def _():
            code_copy(i).start()

    def dest_copy(d):
        return pltpu.make_async_remote_copy(
            src_ref=dests.at[s], dst_ref=dests.at[s],
            send_sem=dest_send.at[d], recv_sem=dest_recv.at[d],
            device_id=(lax.rem(s + d, n), t), device_id_type=MESH)

    @pl.loop(1, n)
    def _(d):
        dest_copy(d).start()

    for i, o in enumerate(OFFSETS):
        @pl.when(jnp.logical_not(has(-o)))
        def _():
            pairs[i + 1] = jnp.zeros(pairs.shape[1:], BF16)
            codes[i + 1] = jnp.zeros(codes.shape[1:], jnp.int32)

    index = merge_index[...] - s * count
    order = jnp.concatenate([index[j:j + 1] for j in range(tp)], axis=1)
    square = (count, count)
    down = lax.broadcasted_iota(jnp.int32, square, 0)
    along = lax.broadcasted_iota(jnp.int32, square, 1)
    diag = down == along
    order_column = jnp.sum(jnp.where(diag, order, 0), axis=1, keepdims=True)
    pick_all = (order_column == along).astype(BF16)
    picks[...] = pick_all

    def column(row):
        return jnp.sum(jnp.where(diag, row, 0), axis=1, keepdims=True)

    gain = first_gain[...].reshape(1, -1)
    gain_column = jnp.transpose(jnp.broadcast_to(gain, (128, gain.shape[1])))[:, 0:1]

    for i in range(2):
        tok_copy(i).wait_recv()
        tok_copy(i + 3).start()
    local[0].wait()
    tok_copy(2).wait_recv()
    for i in range(2):
        tok_copy(i + 3).wait_recv()
    packed = gathered[...].reshape(tp * width, count)
    residual = lax.dot_general(
        picks[pl.ds(pl.multiple_of(t * merged, merged), merged), :], packed,
        (((1,), (1,)), ((), ())), preferred_element_type=F32)
    normed = normalise(packed.astype(F32), gain_column, 0).astype(BF16)
    local[1].wait()
    pairs[0, 0:width] = jnp.dot(wk[...], normed, preferred_element_type=F32).astype(BF16)
    local[2].wait()
    pairs[0, width:2 * width] = jnp.dot(wv[...], normed, preferred_element_type=F32).astype(BF16)
    for i, o in enumerate(OFFSETS):
        @pl.when(has(o))
        def _():
            pair_copy(i).start()

    local[3].wait()
    queries[...] = jnp.dot(wq[...], normed, preferred_element_type=F32).astype(BF16)

    factor = HD ** (-0.5) * LOG2E
    state = [None] * 4
    for b in range(5):
        if b:
            i = b - 1

            @pl.when(has(-OFFSETS[i]))
            def _():
                code_copy(i).wait_recv()
                pair_copy(i).wait_recv()
        allowed = column(codes[b]) == code_query
        if b == 0:
            allowed = allowed | diag
        for h in range(4):
            key = pairs[b, h * HD:(h + 1) * HD]
            value = pairs[b, width + h * HD:width + (h + 1) * HD]
            scores = lax.dot_general(
                key, queries[h * HD:(h + 1) * HD], (((0,), (0,)), ((), ())), preferred_element_type=F32)
            scores = jnp.where(allowed, scores * factor, -1e30)
            top = jnp.max(scores, axis=0, keepdims=True)
            if b:
                top = jnp.maximum(top, state[h][0])
            expo = jnp.exp2(scores - top)
            total = jnp.sum(expo, axis=0, keepdims=True)
            acc = jnp.dot(value, expo.astype(BF16), preferred_element_type=F32)
            if b:
                shrink = jnp.exp2(state[h][0] - top)
                total = total + shrink * state[h][1]
                acc = acc + shrink * state[h][2]
            state[h] = (top, total, acc)

    attended = jnp.concatenate([acc / total for _, total, acc in state], axis=0).astype(BF16)
    attended = lax.dot_general(
        picks[...], attended, (((1,), (1,)), ((), ())), preferred_element_type=F32).astype(BF16)
    local[4].wait()

    def part_copy(i):
        source = part_send.at[(far, beside, across)[i]]
        return pltpu.make_async_remote_copy(
            src_ref=source, dst_ref=part_recv.at[i], send_sem=part_ssem.at[i], recv_sem=part_rsem.at[i],
            device_id=(s, (beside, beside, across)[i]), device_id_type=MESH)

    part = jnp.dot(attended, wo[...], preferred_element_type=F32).astype(BF16)
    for j in range(tp):
        part_send[j] = part[j * merged:(j + 1) * merged]
    part_copy(0).start()
    part_copy(1).start()
    part_copy(0).wait_recv()
    part_send[across] = (part_send[across].astype(F32) + part_recv[0].astype(F32)).astype(BF16)
    part_copy(2).start()
    part_copy(1).wait_recv()
    updated = residual + part_send[t].astype(F32) + part_recv[1].astype(F32)
    part_copy(2).wait_recv()
    updated = updated + part_recv[2].astype(F32)
    merged_norm = normalise(updated, merge_gain[...].reshape(1, -1), 1).astype(BF16)
    local[5].wait()
    proj = jnp.dot(merged_norm, wm[...], preferred_element_type=F32)
    piece = proj.shape[1] // tp
    for j in range(tp):
        proj_send[j] = proj[:, j * piece:(j + 1) * piece].astype(BF16)

    def proj_copy(d):
        peer = lax.rem(t + d, tp)
        return pltpu.make_async_remote_copy(
            src_ref=proj_send.at[peer], dst_ref=proj_recv.at[d],
            send_sem=proj_ssem.at[d], recv_sem=proj_rsem.at[d],
            device_id=(s, peer), device_id_type=MESH)

    for d in range(1, tp):
        proj_copy(d).start()
    projected = proj_send[t].astype(F32)
    for d in range(1, tp):
        proj_copy(d).wait_recv()
        projected = projected + proj_recv[d].astype(F32)
    rows[s] = projected.astype(BF16)

    def row_copy(d):
        return pltpu.make_async_remote_copy(
            src_ref=rows.at[s], dst_ref=rows.at[s],
            send_sem=row_send.at[d], recv_sem=row_recv.at[d],
            device_id=(lax.rem(s + d, n), t), device_id_type=MESH)

    @pl.loop(1, n)
    def _(d):
        row_copy(d).start()

    slot = lax.broadcasted_iota(jnp.int32, (merged, merged), 0)

    def deliver(source):
        one_hot = ((dests[source] - s * merged) == slot).astype(BF16)
        return jnp.dot(one_hot, rows[source], preferred_element_type=F32)

    def step(d, total):
        dest_copy(d).wait_recv()
        row_copy(d).wait_recv()
        return total + deliver(lax.rem(s + n - d, n))

    total = lax.fori_loop(1, n, step, deliver(s))
    out[...] = total.astype(BF16)

    for i in range(5):
        tok_copy(i).wait_send()
    for i in range(3):
        part_copy(i).wait_send()
    for d in range(1, tp):
        proj_copy(d).wait_send()
    for i, o in enumerate(OFFSETS):
        @pl.when(has(o))
        def _():
            code_copy(i).wait_send()
            pair_copy(i).wait_send()

    @pl.loop(1, n)
    def _(d):
        dest_copy(d).wait_send()
        row_copy(d).wait_send()


def body(n, tp, tokens, first_gain, w_query, w_key, w_value, w_out, segment_ids, keep_mask,
         merge_gain, w_merge, merge_index, destination):
    count, width = tokens.shape
    features = w_query.shape[0]
    merged = merge_index.shape[0]
    piece = w_merge.shape[1] // tp
    anywhere = pl.BlockSpec(memory_space=pl.ANY)
    vmem = pl.BlockSpec(memory_space=pltpu.VMEM)
    dma = pltpu.SemaphoreType.DMA
    return pl.pallas_call(
        functools.partial(kernel, n, tp),
        out_shape=jax.ShapeDtypeStruct((merged, piece), BF16),
        in_specs=[anywhere, vmem, anywhere, anywhere, anywhere, anywhere, vmem, vmem, vmem, anywhere, vmem, vmem],
        out_specs=vmem,
        scratch_shapes=[
            pltpu.VMEM((tp, width, count), BF16),
            pltpu.VMEM(w_query.shape[::-1], BF16),
            pltpu.VMEM(w_key.shape[::-1], BF16),
            pltpu.VMEM(w_value.shape[::-1], BF16),
            pltpu.VMEM(w_out.shape, BF16),
            pltpu.VMEM(w_merge.shape, BF16),
            pltpu.VMEM((5, 2 * width, count), BF16),
            pltpu.VMEM((5, 1, count), jnp.int32),
            pltpu.VMEM((n, 1, merged), jnp.int32),
            pltpu.VMEM((width, count), BF16),
            pltpu.VMEM((count, count), BF16),
            pltpu.VMEM((tp, merged, features), BF16),
            pltpu.VMEM((tp, merged, features), BF16),
            pltpu.VMEM((tp, merged, piece), BF16),
            pltpu.VMEM((tp, merged, piece), BF16),
            pltpu.VMEM((n, merged, piece), BF16),
            dma((6,)),
            dma((5,)), dma((5,)),
            dma((4,)), dma((4,)), dma((4,)), dma((4,)),
            dma((n,)), dma((n,)),
            dma((tp,)), dma((tp,)), dma((tp,)), dma((tp,)),
            dma((n,)), dma((n,)),
        ],
        compiler_params=pltpu.CompilerParams(
            collective_id=0, has_side_effects=True, vmem_limit_bytes=56 * 1024 * 1024),
        name="vision_layer",
    )(tokens.T, first_gain, w_query.T, w_key.T, w_value.T, w_out,
      segment_ids.reshape(1, -1), keep_mask.reshape(1, -1), merge_gain,
      w_merge, merge_index.T, destination.reshape(1, -1))


def solution(mesh):
    n, tp = mesh.shape["seq"], mesh.shape["tp"]
    return jax.shard_map(
        functools.partial(body, n, tp),
        mesh=mesh,
        in_specs=(
            P("seq", "tp"), P(), P(None, "tp"), P(None, "tp"), P(None, "tp"), P("tp", None),
            P("seq"), P("seq"), P(), P("tp", None), P("seq", None), P("seq"),
        ),
        out_specs=P("seq", "tp"),
        check_vma=False,
    )
```

time: 66.2 us -> 54.5 us (0.82)
  local copies, waits for them, and re-layouts: 12 us -> 1.38 us
  Pallas kernels: 53.8 us -> 52.8 us
    unnamed x10 -> x1, local copies, waits for them, and re-layouts: 9.39 us -> 1.38 us
    reshape x2 -> x0, local copies, waits for them, and re-layouts: 2.64 us -> none  [the longest x1 1.37 us: body(): first_gain.reshape(1, -1)]
    pallas_call x1, Pallas kernels: 53.8 us -> 52.8 us  [body(): pl.pallas_call(functools.partial(kernel, n, tp), out_shape=jax.ShapeDtype...]
where the time goes in v2:
time: 54.5 us; the launch traced here: 54.2 us
  Pallas kernels  52.8 us (97%)
  local copies, waits for them, and re-layouts  1.38 us (3%)
    pallas_call x1, Pallas kernels, body(): pl.pallas_call(functools.partial(kernel, n, tp), out_shape=jax.ShapeDtype...  52.8 us
    unnamed x1, local copies, waits for them, and re-layouts  1.38 us

profile of v2, /device:TPU:0, one launch (start us, length us, event | category | flops | bytes accessed | tf_op | source)
XLA Modules:
  0.0 54.2 jit_solution(17362493361717999870)
XLA Ops:
  0.0 52.8 %vision_layer.1 = bf16[64,160]{1,0:T(8,128)(2,1)} custom-call(bf16[320,256]{1,0:T(8,128)(2,1)} %bitcast.11, f32[1280]{0:T(1024)} %first_gain.1, bf16[320,1280]{1,0:T(8,128)(2,1)} %bitcast.8, bf16[320,1280]{1,0:T(8,128)(2,1)} %bitcast.9, bf16[320,1280]{1,0:T(8,128)(2,1)} %bitcast.10, bf16[320,1280]{1,0:T(8,128)(2,1)} %w_out.1, s32[1,256]{1,0:T(1,128)} %bitcast.13, ...), custom_call_target="tpu_custom_call" | custom-call | tf_op jit(solution)/shard_map/vision_layer/pallas_call | solution.py:287
  52.8 1.4 %copy.14 = bf16[64,160]{1,0:T(8,128)(2,1)} copy(bf16[64,160]{1,0:T(8,128)(2,1)} %vision_layer.1) | data formatting | bytes 40960

commit v3 on v2

--- a/solution.py
+++ b/solution.py
@@ -11,6 +11,7 @@
 EPS = 1e-06
 LOG2E = 1.4426950408889634
 MESH = pl.DeviceIdType.MESH
+BLOCK = 16
 OFFSETS = (1, -1, 2, -2)
 F32 = jnp.float32
 BF16 = jnp.bfloat16
@@ -29,7 +30,7 @@
     merge_gain, w_merge, merge_index, destination,
     out,
     gathered, wq, wk, wv, wo, wm, pairs, codes, dests, queries,
-    picks, part_send, part_recv, proj_send, proj_recv, rows,
+    picks, part_send, part_recv, proj_send, proj_recv, sort, spread, leaving, rows,
     local_sem, tok_send, tok_recv, pair_send, pair_recv, code_send, code_recv,
     dest_send, dest_recv, part_ssem, part_rsem, proj_ssem, proj_rsem, row_send, row_recv,
 ):
@@ -156,6 +157,36 @@
 
     local[3].wait()
     queries[...] = jnp.dot(wq[...], normed, preferred_element_type=F32).astype(BF16)
+
+    small = (merged, merged)
+    first = lax.broadcasted_iota(jnp.int32, small, 0)
+    second = lax.broadcasted_iota(jnp.int32, small, 1)
+
+    def places(row):
+        owner = jnp.floor(row.astype(F32) * (1.0 / merged))
+        owner_column = jnp.sum(jnp.where(first == second, owner, 0.0), axis=1, keepdims=True)
+        before = (owner_column == owner) & (first < second)
+        return owner, jnp.sum(jnp.where(before, 1.0, 0.0), axis=0, keepdims=True)
+
+    owner, rank = places(dests[s])
+    block_row = lax.broadcasted_iota(jnp.int32, sort.shape, 0).astype(F32)
+    sort[...] = (owner * BLOCK + rank == block_row).astype(BF16)
+    in_block = lax.broadcasted_iota(jnp.int32, (BLOCK, merged), 0).astype(F32)
+
+    def place(source):
+        row = dests[source]
+        owner, rank = places(row)
+        here = ((owner == s.astype(F32)) & (rank == in_block)).astype(BF16)
+        slots = ((row - s * merged) == first).astype(BF16)
+        spread[source] = lax.dot_general(
+            here, slots, (((1,), (1,)), ((), ())), preferred_element_type=F32).astype(BF16)
+
+    place(s)
+
+    @pl.loop(1, n)
+    def _(d):
+        dest_copy(d).wait_recv()
+        place(lax.rem(s + n - d, n))
 
     factor = HD ** (-0.5) * LOG2E
     state = [None] * 4
@@ -231,31 +262,29 @@
     for d in range(1, tp):
         proj_copy(d).wait_recv()
         projected = projected + proj_recv[d].astype(F32)
-    rows[s] = projected.astype(BF16)
+    sorted_rows = jnp.dot(sort[...], projected.astype(BF16), preferred_element_type=F32).astype(BF16)
+    leaving[...] = sorted_rows.reshape(leaving.shape)
 
     def row_copy(d):
-        return pltpu.make_async_remote_copy(
-            src_ref=rows.at[s], dst_ref=rows.at[s],
+        peer = lax.rem(s + d, n)
+        return pltpu.make_async_remote_copy(
+            src_ref=leaving.at[peer], dst_ref=rows.at[s],
             send_sem=row_send.at[d], recv_sem=row_recv.at[d],
-            device_id=(lax.rem(s + d, n), t), device_id_type=MESH)
+            device_id=(peer, t), device_id_type=MESH)
 
     @pl.loop(1, n)
     def _(d):
         row_copy(d).start()
 
-    slot = lax.broadcasted_iota(jnp.int32, (merged, merged), 0)
-
-    def deliver(source):
-        one_hot = ((dests[source] - s * merged) == slot).astype(BF16)
-        return jnp.dot(one_hot, rows[source], preferred_element_type=F32)
-
-    def step(d, total):
-        dest_copy(d).wait_recv()
+    rows[s] = leaving[s]
+
+    @pl.loop(1, n)
+    def _(d):
         row_copy(d).wait_recv()
-        return total + deliver(lax.rem(s + n - d, n))
-
-    total = lax.fori_loop(1, n, step, deliver(s))
-    out[...] = total.astype(BF16)
+
+    out[...] = lax.dot_general(
+        spread[...].reshape(n * BLOCK, merged), rows[...].reshape(n * BLOCK, piece),
+        (((0,), (0,)), ((), ())), preferred_element_type=F32).astype(BF16)
 
     for i in range(5):
         tok_copy(i).wait_send()
@@ -305,7 +334,10 @@
             pltpu.VMEM((tp, merged, features), BF16),
             pltpu.VMEM((tp, merged, piece), BF16),
             pltpu.VMEM((tp, merged, piece), BF16),
-            pltpu.VMEM((n, merged, piece), BF16),
+            pltpu.VMEM((n * BLOCK, merged), BF16),
+            pltpu.VMEM((n, BLOCK, merged), BF16),
+            pltpu.VMEM((n, BLOCK, piece), BF16),
+            pltpu.VMEM((n, BLOCK, piece), BF16),
             dma((6,)),
             dma((5,)), dma((5,)),
             dma((4,)), dma((4,)), dma((4,)), dma((4,)),

time: 54.5 us -> 52.8 us (0.969)
  Pallas kernels: 52.8 us -> 51.2 us
    pallas_call x1, Pallas kernels: 52.8 us -> 51.2 us  [body(): pl.pallas_call(functools.partial(kernel, n, tp), out_shape=jax.ShapeDtype...]
where the time goes in v3:
time: 52.8 us; the launch traced here: 52.6 us
  Pallas kernels  51.2 us (97%)
  local copies, waits for them, and re-layouts  1.38 us (3%)
    pallas_call x1, Pallas kernels, body(): pl.pallas_call(functools.partial(kernel, n, tp), out_shape=jax.ShapeDtype...  51.2 us
    unnamed x1, local copies, waits for them, and re-layouts  1.38 us

profile of v3, /device:TPU:0, one launch (start us, length us, event | category | flops | bytes accessed | tf_op | source)
XLA Modules:
  0.0 52.6 jit_solution(28043578351541572)
XLA Ops:
  0.0 51.2 %vision_layer.1 = bf16[64,160]{1,0:T(8,128)(2,1)} custom-call(bf16[320,256]{1,0:T(8,128)(2,1)} %bitcast.11, f32[1280]{0:T(1024)} %first_gain.1, bf16[320,1280]{1,0:T(8,128)(2,1)} %bitcast.8, bf16[320,1280]{1,0:T(8,128)(2,1)} %bitcast.9, bf16[320,1280]{1,0:T(8,128)(2,1)} %bitcast.10, bf16[320,1280]{1,0:T(8,128)(2,1)} %w_out.1, s32[1,256]{1,0:T(1,128)} %bitcast.13, ...), custom_call_target="tpu_custom_call" | custom-call | tf_op jit(solution)/shard_map/vision_layer/pallas_call | solution.py:316
  51.2 1.4 %copy.14 = bf16[64,160]{1,0:T(8,128)(2,1)} copy(bf16[64,160]{1,0:T(8,128)(2,1)} %vision_layer.1) | data formatting | bytes 40960
